TPU v7x, 256 devices: a whole 4x4x8 slice. The times are simulated.
256 devices in a mesh: seq: 8 (over z), fsdp: 32 (over y, x, core).
Axes of the slice: x: 4, y: 4, z: 8, core: 2. Of those that a mesh axis runs over, the one named last changes fastest.
Arguments:
- tokens: bfloat16 [4096, 4096], P('seq', 'fsdp'), may hold values from -6 to 6
- in_mask: int32 [4096, 4096], P('seq', 'fsdp'), may hold values 0 or 1
- out_mask: int32 [4096, 32, 384], P('seq', 'fsdp'), may hold values 0 or 1
- w_mean: bfloat16 [4096, 32, 384], P('seq', 'fsdp'), may hold values from -0.09375 to 0.09375
- w_sigma: bfloat16 [4096, 32, 384], P('seq', 'fsdp'), may hold values from -0.046875 to 0.046875
- grad_out: bfloat16 [4096, 4096], P('seq', 'fsdp'), may hold values from -6 to 6
Outputs:
- attended: bfloat16 [4096, 4096], P('seq', 'fsdp')
- d_tokens: bfloat16 [4096, 4096], P('seq', 'fsdp')
- g_mean: bfloat16 [4096, 32, 384], P('seq', 'fsdp')
- g_sigma: bfloat16 [4096, 32, 384], P('seq', 'fsdp')
Inputs may be any that keep to these rules, and one draw needn't show every extreme that they name: `in_mask`: each entry is a sign bit: the sign is 2 * entry - 1. `out_mask`: each entry is a sign bit: the sign is 2 * entry - 1.
All inputs are finite; a program needn't handle non-finite values. No bound on the sum of `in_mask` or of `out_mask` on one device may be relied on, other than what follows from the above.
Results may differ from a plain program's by a relative error of at most 0.017.
Values may be sent and summed in bfloat16 or wider, within the bound.
A program may use at most 64 MiB of HBM per device.

v0:
```python
import jax
import jax.numpy as jnp
from jax import lax
from jax.sharding import PartitionSpec as P

EPSILON = 1e-06


def prefix(shard, axis, join, neutral):
    place = lax.axis_index(axis)
    gathered = lax.all_gather(shard.astype(jnp.bfloat16), axis)
    state = jnp.zeros_like(shard) + jnp.asarray(neutral, shard.dtype)

    def one(hop, state):
        return join(state, lax.dynamic_index_in_dim(gathered, hop, 0, False).astype(shard.dtype))

    return lax.fori_loop(0, place, one, state)


def carried_in(shard, axis, combine, identity):
    devices, mine = (lax.axis_size(axis), lax.axis_index(axis))
    everything = lax.all_gather(
        shard.astype(jnp.bfloat16 if shard.dtype == jnp.float32 else shard.dtype), axis
    )
    start = jnp.broadcast_to(jnp.asarray(identity, shard.dtype), shard.shape)

    def hop(k, before):
        at = devices - 1 - k
        reached = at > mine
        new = combine(before, everything[at].astype(shard.dtype))
        return jnp.where(reached, new, before)

    return lax.fori_loop(0, devices, hop, start)


def feature_map(u):
    return jnp.where(u > 0, u + 1.0, jnp.exp(jnp.minimum(u, 0.0)))


def feature_slope(u):
    return jnp.where(u > 0, 1.0, jnp.exp(jnp.minimum(u, 0.0)))


def local(tokens, in_mask, out_mask, w_mean, w_sigma, grad_out):
    highest = lax.Precision.HIGHEST
    tok_rows = tokens.shape[0]
    head_count = w_mean.shape[1]
    head_width = w_mean.shape[2] // 3
    in_sign = (2 * in_mask - 1).astype(jnp.bfloat16)
    flipped = tokens * in_sign
    gathered, gathered_flip = (
        lax.all_gather(tokens, "fsdp", axis=1, tiled=True),
        lax.all_gather(flipped, "fsdp", axis=1, tiled=True),
    )
    panel_mean, panel_sigma = (
        lax.all_gather(w_mean, "seq", axis=0, tiled=True),
        lax.all_gather(w_sigma, "seq", axis=0, tiled=True),
    )
    out_sign = (2 * out_mask - 1).astype(jnp.bfloat16)
    sign_heads = jnp.transpose(out_sign, (1, 0, 2)).astype(jnp.float32)
    projected = jnp.einsum("td,dhc->htc", gathered, panel_mean, preferred_element_type=jnp.float32)
    projected = (
        projected
        + jnp.einsum("td,dhc->htc", gathered_flip, panel_sigma, preferred_element_type=jnp.float32)
        * sign_heads
    )
    pre_query = projected[:, :, :head_width]
    pre_keys = projected[:, :, head_width : 2 * head_width]
    queries = feature_map(pre_query)
    key_feats = feature_map(pre_keys)
    values = projected[:, :, 2 * head_width :]
    causal = (
        lax.broadcasted_iota(jnp.int32, (tok_rows, tok_rows), 0)
        >= lax.broadcasted_iota(jnp.int32, (tok_rows, tok_rows), 1)
    ).astype(jnp.float32)
    local_state = jnp.einsum("hse,hsf->hef", key_feats, values, precision=highest)
    incoming = prefix(local_state, "seq", jnp.add, jnp.zeros_like(local_state))
    scores = jnp.einsum("hte,hse->hts", queries, key_feats, precision=highest) * causal
    numerator = jnp.einsum("hts,hsf->htf", scores, values, precision=highest)
    numerator = numerator + jnp.einsum("hte,hef->htf", queries, incoming, precision=highest)
    inv_norm = lax.rsqrt(jnp.mean(numerator * numerator, axis=-1, keepdims=True) + EPSILON)
    normed = numerator * inv_norm
    attended = (
        jnp.transpose(normed, (1, 0, 2))
        .reshape(tok_rows, head_count * head_width)
        .astype(jnp.bfloat16)
    )
    upstream = jnp.transpose(
        grad_out.astype(jnp.float32).reshape(tok_rows, head_count, head_width), (1, 0, 2)
    )
    d_numer = inv_norm * (upstream - normed * jnp.mean(upstream * normed, axis=-1, keepdims=True))
    local_back = jnp.einsum("hte,htf->hef", queries, d_numer, precision=highest)
    suffix = carried_in(local_back, "seq", jnp.add, jnp.zeros_like(local_back))
    d_scores = jnp.einsum("htf,hsf->hts", d_numer, values, precision=highest) * causal
    d_query = jnp.einsum("hts,hse->hte", d_scores, key_feats, precision=highest)
    d_query = d_query + jnp.einsum("hef,htf->hte", incoming, d_numer, precision=highest)
    d_keys = jnp.einsum("hts,hte->hse", d_scores, queries, precision=highest)
    d_keys = d_keys + jnp.einsum("hef,hsf->hse", suffix, values, precision=highest)
    d_values = jnp.einsum("hts,htf->hsf", scores, d_numer, precision=highest)
    d_values = d_values + jnp.einsum("hef,hse->hsf", suffix, key_feats, precision=highest)
    grad_pre = jnp.concatenate(
        [d_query * feature_slope(pre_query), d_keys * feature_slope(pre_keys), d_values], axis=-1
    )
    grad_mean = jnp.transpose(grad_pre, (1, 0, 2)).astype(jnp.bfloat16)
    grad_sigma = grad_mean * out_sign
    part_mean = jnp.einsum("td,thc->dhc", gathered, grad_mean, preferred_element_type=jnp.float32)
    part_sigma = jnp.einsum(
        "td,thc->dhc", gathered_flip, grad_sigma, preferred_element_type=jnp.float32
    )
    sum_mean, sum_sigma = (
        lax.psum_scatter(
            part_mean.astype(jnp.bfloat16), "seq", scatter_dimension=0, tiled=True
        ).astype(jnp.float32),
        lax.psum_scatter(
            part_sigma.astype(jnp.bfloat16), "seq", scatter_dimension=0, tiled=True
        ).astype(jnp.float32),
    )
    panel_mean, panel_sigma = (
        lax.all_gather(w_mean, "seq", axis=0, tiled=True),
        lax.all_gather(w_sigma, "seq", axis=0, tiled=True),
    )
    back_mean = jnp.einsum("thc,dhc->td", grad_mean, panel_mean, preferred_element_type=jnp.float32)
    back_sigma = jnp.einsum(
        "thc,dhc->td", grad_sigma, panel_sigma, preferred_element_type=jnp.float32
    )
    own_mean, own_sigma = (
        lax.psum_scatter(
            back_mean.astype(jnp.bfloat16), "fsdp", scatter_dimension=1, tiled=True
        ).astype(jnp.float32),
        lax.psum_scatter(
            back_sigma.astype(jnp.bfloat16), "fsdp", scatter_dimension=1, tiled=True
        ).astype(jnp.float32),
    )
    d_tokens = (own_mean + in_sign.astype(jnp.float32) * own_sigma).astype(jnp.bfloat16)
    return (attended, d_tokens, sum_mean.astype(jnp.bfloat16), sum_sigma.astype(jnp.bfloat16))


def solution(mesh):
    placed = (
        P("seq", "fsdp"),
        P("seq", "fsdp"),
        P("seq", "fsdp", None),
        P("seq", "fsdp", None),
        P("seq", "fsdp", None),
        P("seq", "fsdp"),
    )
    return jax.shard_map(
        local,
        mesh=mesh,
        in_specs=placed,
        out_specs=(
            P("seq", "fsdp"),
            P("seq", "fsdp"),
            P("seq", "fsdp", None),
            P("seq", "fsdp", None),
        ),
        check_vma=False,
    )
```

profile of v0, /device:TPU:4, one launch (start us, length us, event | category | flops | bytes accessed | tf_op | source)
XLA Modules:
  0.0 579.9 jit_solution(4154613586621384523)
XLA Ops:
  7.2 0.7 all-gather.13.cloned.1.call-update
  7.9 1.7 fusion.49
  9.7 0.0 all-gather.7.cloned.1.call-start
  9.8 0.7 all-gather.7.cloned.1.call-update
  10.5 0.5 all-gather.9.cloned.1.call-update
  11.1 1.0 copy.18
  12.1 2.2 copy.16
  14.3 43.4 %all-gather.13.cloned.1.call-done = bf16[4096,1,384]{2,0,1:T(8,128)(2,1)} async-done(((bf16[512,1,384]{2,0,1:T(8,128)(2,1)}), bf16[4096,1,384]{2,0,1:T(8,128)(2,1)}) %all-gather.13.cloned.1.call-update) | async-done | bytes 3145744 | tf_op jit(solution)/shard_map/all_gather | solution.py:57
  57.7 54.6 %all-gather.11.cloned.1.call-done = bf16[512,4096]{1,0:T(8,128)(2,1)} async-done(((bf16[512,128]{1,0:T(8,128)(2,1)}), bf16[512,4096]{1,0:T(8,128)(2,1)}) %all-gather.11.cloned.1.call-update) | async-done | bytes 4194320 | tf_op jit(solution)/shard_map/all_gather | solution.py:53
  112.3 5.0 fusion.14
  117.3 42.8 %all-gather.7.cloned.1.call-done = bf16[4096,1,384]{2,0,1:T(8,128)(2,1)} async-done(((bf16[512,1,384]{2,0,1:T(8,128)(2,1)}), bf16[4096,1,384]{2,0,1:T(8,128)(2,1)}) %all-gather.7.cloned.1.call-update) | async-done | bytes 3145744 | tf_op jit(solution)/shard_map/all_gather | solution.py:56
  160.1 53.8 %all-gather.9.cloned.1.call-done = bf16[512,4096]{1,0:T(8,128)(2,1)} async-done(((bf16[512,128]{1,0:T(8,128)(2,1)}), bf16[512,4096]{1,0:T(8,128)(2,1)}) %all-gather.9.cloned.1.call-update) | async-done | bytes 4194320 | tf_op jit(solution)/shard_map/all_gather | solution.py:52
  213.9 5.0 fusion.17
  218.9 0.1 slice_compare_fusion
  219.0 0.4 convolution_convert_fusion.5
  219.4 26.3 %all-gather = bf16[1024,128]{1,0:T(8,128)(2,1)S(1)} all-gather(bf16[128,128]{1,0:T(8,128)(2,1)S(1)} %convolution_convert_fusion.5), channel_id=2, replica_groups=mesh['seq'=8,'fsdp'=32] {'seq'}, dimensions={0}, use_global_device_ids=true | all-gather | bytes 294912 | tf_op jit(solution)/shard_map/all_gather | solution.py:11
  245.7 1.1 convolution_select_fusion.1
  246.8 1.2 fusion.44
  248.0 0.5 multiply_reduce_fusion
  248.5 0.1 fusion.32
  248.6 0.7 fusion.51
  249.3 0.4 convolution_convert_fusion.4
  249.8 1.0 convolution_select_fusion
  250.8 0.8 fusion.40
  251.6 1.2 fusion.35
  252.8 25.0 %all-gather.1 = bf16[1024,128]{1,0:T(8,128)(2,1)S(1)} all-gather(bf16[128,128]{1,0:T(8,128)(2,1)S(1)} %convolution_convert_fusion.4), channel_id=3, replica_groups=mesh['seq'=8,'fsdp'=32] {'seq'}, dimensions={0}, use_global_device_ids=true | all-gather | bytes 294912 | tf_op jit(solution)/shard_map/all_gather | solution.py:22
  277.8 0.4 while.27
  278.2 0.5 fusion.22
  278.7 0.5 convolution_add_fusion
  279.2 0.4 fusion.23
  279.6 6.3 %convolution_convert_fusion = bf16[512,4096]{1,0:T(8,128)(2,1)} fusion(bf16[4096,1,384]{2,0,1:T(8,128)(2,1)} %all-gather.13.cloned.1.call-done, s32[512,1,384]{0,2,1:T(8,128)S(1)} %copy.16, bf16[1,512,128]{1,2,0:T(8,128)(2,1)S(1)} %bitcast.145, bf16[1,512,128]{1,2,0:T(8,128)(2,1)S(1)} %fusion.23, bf16[1,512,128]{1,2,0:T(8,128)(2,1)S(1)} %fusion.22), kind=kOutput, calls=%fused_computation.2 | convolution fusion | flops 1615265792 | bytes 8519680 | tf_op jit(solution)/shard_map/thc,dhc->td/dot_general | solution.py:123
  285.9 6.5 %copy.24 = bf16[512,4096]{0,1:T(8,128)(2,1)} copy(bf16[512,4096]{1,0:T(8,128)(2,1)} %convolution_convert_fusion) | data formatting | bytes 8388608
  292.4 0.0 reduce-scatter.13.cloned.1.call-start
  292.4 6.2 %convolution_convert_fusion.1 = bf16[512,4096]{1,0:T(8,128)(2,1)} fusion(bf16[4096,1,384]{2,0,1:T(8,128)(2,1)} %all-gather.7.cloned.1.call-done, bf16[512,128]{0,1:T(8,128)(2,1)S(1)} %convolution_add_fusion, bf16[512,128]{0,1:T(8,128)(2,1)S(1)} %bitcast.148, bf16[512,128]{0,1:T(8,128)(2,1)S(1)} %bitcast.142), kind=kOutput, calls=%fused_computation.3 | convolution fusion | flops 1613889536 | bytes 7733248 | tf_op jit(solution)/shard_map/thc,dhc->td/dot_general | solution.py:122
  298.6 6.5 %copy.22 = bf16[512,4096]{0,1:T(8,128)(2,1)} copy(bf16[512,4096]{1,0:T(8,128)(2,1)} %convolution_convert_fusion.1) | data formatting | bytes 8388608
  305.1 0.0 reduce-scatter.9.cloned.1.call-start
  305.2 5.8 fusion
  311.0 0.0 reduce-scatter.11.cloned.1.call-start
  311.0 6.4 %fusion.1 = bf16[4096,1,384]{2,0,1:T(8,128)(2,1)} fusion(bf16[512,4096]{1,0:T(8,128)(2,1)} %all-gather.11.cloned.1.call-done, s32[512,1,384]{0,2,1:T(8,128)S(1)} %copy.16, bf16[1,512,128]{1,2,0:T(8,128)(2,1)S(1)} %bitcast.147, bf16[1,512,128]{1,2,0:T(8,128)(2,1)S(1)} %fusion.23, bf16[1,512,128]{1,2,0:T(8,128)(2,1)S(1)} %fusion.22), kind=kOutput, calls=%fused_computation.7 | convolution fusion | flops 1614741504 | bytes 8519680 | tf_op jit(solution)/shard_map/td,thc->dhc/dot_general | solution.py:107
  317.5 0.8 copy.20
  318.2 63.1 %reduce-scatter.15.cloned.1.call-done = bf16[128,512]{1,0:T(8,128)(2,1)} async-done(((bf16[4096,512]{1,0:T(8,128)(2,1)}), bf16[128,512]{1,0:T(8,128)(2,1)}) %reduce-scatter.15.cloned.1.call-update) | async-done | bytes 131088
  381.3 1.0 copy.25
  382.4 92.3 %reduce-scatter.13.cloned.1.call-done = bf16[128,512]{1,0:T(8,128)(2,1)} async-done(((bf16[4096,512]{1,0:T(8,128)(2,1)}), bf16[128,512]{1,0:T(8,128)(2,1)}) %reduce-scatter.13.cloned.1.call-update) | async-done | bytes 131088
  474.7 1.0 copy.23
  475.7 47.9 %reduce-scatter.9.cloned.1.call-done = bf16[512,1,384]{0,2,1:T(8,128)(2,1)} async-done(((bf16[4096,1,384]{0,2,1:T(8,128)(2,1)}), bf16[512,1,384]{0,2,1:T(8,128)(2,1)}) %reduce-scatter.9.cloned.1.call-update) | async-done | bytes 393232 | tf_op jit(solution)/shard_map/reduce_scatter | solution.py:111
  523.6 1.9 copy.21
  525.6 0.7 add_convert_fusion.1
  526.3 46.8 %reduce-scatter.11.cloned.1.call-done = bf16[512,1,384]{2,0,1:T(8,128)(2,1)} async-done(((bf16[4096,1,384]{2,0,1:T(8,128)(2,1)}), bf16[512,1,384]{2,0,1:T(8,128)(2,1)}) %reduce-scatter.11.cloned.1.call-update) | async-done | bytes 393232 | tf_op jit(solution)/shard_map/reduce_scatter | solution.py:114
  (24 shorter events, 0.4 us)
Async XLA Ops:
  7.2 50.6 %all-gather.13.cloned.1.call-start = ((), (), s32[]{:S(2)}) async-start(), calls=%async_computation.7 | async-start | bytes 3538944 | tf_op jit(solution)/shard_map/all_gather | solution.py:57
  7.9 104.4 %all-gather.11.cloned.1.call-start = ((), (), s32[]{:S(2)}) async-start(), calls=%async_computation.6 | async-start | bytes 4325376 | tf_op jit(solution)/shard_map/all_gather | solution.py:53
  9.7 150.4 %all-gather.7.cloned.1.call-start = ((), (), s32[]{:S(2)}) async-start(), calls=%async_computation.4 | async-start | bytes 3538944 | tf_op jit(solution)/shard_map/all_gather | solution.py:56
  10.4 203.5 %all-gather.9.cloned.1.call-start = ((), (), s32[]{:S(2)}) async-start(), calls=%async_computation.5 | async-start | bytes 4325376 | tf_op jit(solution)/shard_map/all_gather | solution.py:52
  11.0 370.3 %reduce-scatter.15.cloned.1.call-start = ((), (), s32[]{:S(2)}) async-start(), calls=%async_computation.11 | async-start | bytes 4325376
  292.4 182.3 %reduce-scatter.13.cloned.1.call-start = ((), (), s32[]{:S(2)}) async-start(), calls=%async_computation.10 | async-start | bytes 4325376
  305.1 218.5 %reduce-scatter.9.cloned.1.call-start = ((), (), s32[]{:S(2)}) async-start(), calls=%async_computation.8 | async-start | bytes 3538944 | tf_op jit(solution)/shard_map/reduce_scatter | solution.py:111
  311.0 262.1 %reduce-scatter.11.cloned.1.call-start = ((), (), s32[]{:S(2)}) async-start(), calls=%async_computation.9 | async-start | bytes 3538944 | tf_op jit(solution)/shard_map/reduce_scatter | solution.py:114
  317.4 208.1 %copy-start = (s32[512,128]{1,0:T(8,128)S(1)}, s32[512,128]{1,0:T(8,128)}, u32[]{:S(2)}) copy-start(s32[512,128]{1,0:T(8,128)} %param.11) | copy-start | bytes 786436
Sparse Core Ops, SparseCore 0:
  9.8 47.9 all-gather.12
  60.8 51.4 all-gather.10
  114.1 45.9 all-gather.6
  162.4 51.4 all-gather.8
  292.5 88.7 reduce-scatter.14
  385.6 88.9 reduce-scatter.12
  477.2 46.3 reduce-scatter.8
  526.8 46.2 reduce-scatter.10
where the time goes:
time: 581 us; the launch traced here: 580 us
  waiting for transfers between devices  447 us (77%)
  blocking collectives  51.3 us (9%)
  matrix products  43.4 us (7%)
  local copies, waits for them, and re-layouts  20.9 us (4%)
  between operations  14.3 us (2%)
    unnamed x10, waiting for transfers between devices  157 us
    all_gather x1, waiting for transfers between devices, local(): lax.all_gather(flipped, 'fsdp', axis=1, tiled=True)  54.6 us
    all_gather x1, waiting for transfers between devices, local(): lax.all_gather(tokens, 'fsdp', axis=1, tiled=True)  53.8 us
    reduce_scatter x1, waiting for transfers between devices, local(): lax.psum_scatter(part_mean.astype(jnp.bfloat16), 'seq', scatter_dimension...  47.9 us
    reduce_scatter x1, waiting for transfers between devices, local(): lax.psum_scatter(part_sigma.astype(jnp.bfloat16), 'seq', scatter_dimensio...  46.8 us
    all_gather x1, waiting for transfers between devices, local(): lax.all_gather(w_sigma, 'seq', axis=0, tiled=True)  43.4 us
    all_gather x1, waiting for transfers between devices, local(): lax.all_gather(w_mean, 'seq', axis=0, tiled=True)  42.8 us
    all_gather x1, blocking collectives, prefix(): gathered = lax.all_gather(shard.astype(jnp.bfloat16), axis)  26.3 us
  transfers between devices with their start and end apart: 8, of which 8 were waited for; matrix products, arithmetic and copies ran while one was open for 7% of the time, Pallas kernels for 0%

commit v1 on v0

v1 whole, which is shorter than its diff:
```python
import jax
import jax.numpy as jnp
from jax import lax
from jax.experimental import pallas as pl
from jax.experimental.pallas import tpu as pltpu
from jax.sharding import PartitionSpec as P

EPSILON = 1e-06
MESH = pl.DeviceIdType.MESH
F32 = jnp.float32
BF16 = jnp.bfloat16
TB = 512
DB = 128
KB = 512
E = 128
C = 3 * E
NZ = 8
HALF = TB // 2


def nn(a, b):
    return lax.dot_general(a, b, (((1,), (0,)), ((), ())), preferred_element_type=F32)


def nt(a, b):
    return lax.dot_general(a, b, (((1,), (1,)), ((), ())), preferred_element_type=F32)


def kernel(
    tok, in_mask, sgn, w_mean, w_sigma, gout,
    att_out, dtok_out, gm_out, gs_out,
    ta, sa, w_all, pm, ps, sts, str_, sus, sur, inc, suf, sc, sct, ds, dst, nu, dki, dvi,
    gb, gsb, gt, gst, gp, rr, bp, cr, xr, yr, xb, yb, xr2, yr2,
    zs, zr, ts, tr, ss, sr, cs, crs, st_s, st_r, su_s, su_r, rs_s, rs_r, bc_s, bc_r, bx_s, bx_r, by_s, by_r,
):
    s = lax.axis_index("seq")
    f = lax.axis_index("fsdp")
    c = lax.rem(f, 2)
    x = lax.rem(lax.div(f, 2), 4)
    y = lax.div(f, 8)
    oc = 1 - c

    def at_seq(k):
        return (lax.rem(s + k, NZ), f)

    def at_x(k):
        return (s, (y * 4 + lax.rem(x + k, 4)) * 2 + c)

    def at_y(k):
        return (s, (lax.rem(y + k, 4) * 4 + x) * 2 + c)

    partner = (s, (y * 4 + x) * 2 + oc)
    pending = []

    def copy(src, dst, send, recv, dev):
        return pltpu.make_async_remote_copy(
            src_ref=src, dst_ref=dst, send_sem=send, recv_sem=recv, device_id=dev, device_id_type=MESH
        )

    def start(src, dst, send, recv, dev):
        one = copy(src, dst, send, recv, dev)
        one.start()
        pending.append(one)

    def arrived(ref, send, recv):
        copy(ref, ref, send, recv, partner).wait_recv()

    barrier = pltpu.get_barrier_semaphore()
    peers = [at_seq(k) for k in range(1, NZ)] + [at_x(k) for k in (1, 2, 3)] + [at_y(k) for k in (1, 2, 3)] + [partner]
    for peer in peers:
        pl.semaphore_signal(barrier, inc=1, device_id=peer, device_id_type=MESH)

    ta[c, y, x] = tok[...]
    sa[c, y, x] = (2 * in_mask[...] - 1).astype(F32).astype(BF16)
    w_all[s, 0] = w_mean[...]
    w_all[s, 1] = w_sigma[...]
    pl.semaphore_wait(barrier, len(peers))

    def ring_out(way, hop, m):
        owner = lax.rem(s + (NZ - hop if way == 0 else hop), NZ)
        ref = w_all.at[owner, m]
        start(ref, ref, zs.at[way, hop, m], zr.at[way, hop, m], at_seq(1 if way == 0 else NZ - 1))

    def ring_in(way, hop, m):
        owner = lax.rem(s + (NZ - 1 - hop if way == 0 else 1 + hop), NZ)
        arrived(w_all.at[owner, m], zs.at[way, hop, m], zr.at[way, hop, m])

    def ring_step(hop, part):
        for way in (0, 1):
            m = part if way == 0 else 1 - part
            ring_in(way, hop, m)
            if hop < 2 or (hop == 2 and part == 0):
                ring_out(way, hop + 1, m)

    for part in (0, 1):
        ring_out(0, 0, part)
        ring_out(1, 0, 1 - part)

    for k in (1, 2, 3):
        start(ta.at[c, y, x], ta.at[c, y, x], ts.at[k - 1], tr.at[k - 1], at_x(k))
        start(sa.at[c, y, x], sa.at[c, y, x], ss.at[k - 1], sr.at[k - 1], at_y(k))
    for k in (1, 2, 3):
        arrived(ta.at[c, y, lax.rem(x + 4 - k, 4)], ts.at[k - 1], tr.at[k - 1])
    for k in (1, 2, 3):
        start(ta.at[c, y], ta.at[c, y], ts.at[2 + k], tr.at[2 + k], at_y(k))
    for k in (1, 2, 3):
        arrived(sa.at[c, lax.rem(y + 4 - k, 4), x], ss.at[k - 1], sr.at[k - 1])
    for k in (1, 2, 3):
        start(sa.at[c, :, x], sa.at[c, :, x], ss.at[2 + k], sr.at[2 + k], at_x(k))
    start(ta.at[c, y], ta.at[c, y], cs.at[0], crs.at[0], partner)
    start(sa.at[c, :, x], sa.at[c, :, x], cs.at[4], crs.at[4], partner)

    ring_step(0, 0)
    ring_step(0, 1)
    ring_step(1, 0)
    for k in (1, 2, 3):
        yk = lax.rem(y + 4 - k, 4)
        arrived(ta.at[c, yk], ts.at[2 + k], tr.at[2 + k])
        start(ta.at[c, yk], ta.at[c, yk], cs.at[k], crs.at[k], partner)
        xk = lax.rem(x + 4 - k, 4)
        arrived(sa.at[c, :, xk], ss.at[2 + k], sr.at[2 + k])
        start(sa.at[c, :, xk], sa.at[c, :, xk], cs.at[4 + k], crs.at[4 + k], partner)
    ring_step(1, 1)
    for k in range(4):
        arrived(ta.at[oc, lax.rem(y + 4 - k, 4)], cs.at[k], crs.at[k])
        arrived(sa.at[oc, :, lax.rem(x + 4 - k, 4)], cs.at[4 + k], crs.at[4 + k])

    def columns(ref, e):
        row, first = lax.div(e, 2), 2 * lax.rem(e, 2)
        return jnp.concatenate([ref[j % 2, row, first + j // 2] for j in range(4)], axis=1)

    pm[...] = jnp.zeros_like(pm)
    ps[...] = jnp.zeros_like(ps)

    def project(first, stride, count):
        def one(i, carry):
            owner = lax.rem(s + first + i * stride, NZ)
            t = columns(ta, owner)
            pm[...] += nn(t, w_all[owner, 0])
            ps[...] += nn(t * columns(sa, owner), w_all[owner, 1])
            return carry

        lax.fori_loop(0, count, one, 0)

    project(NZ - 2, 1, 5)
    ring_step(2, 0)
    ring_step(2, 1)
    project(NZ - 3, 6, 2)
    ring_in(0, 3, 0)
    ring_in(1, 3, 1)
    project(4, 1, 1)

    so = sgn[...].astype(F32)
    pre = pm[...] + ps[...] * so
    uq, uk, v = pre[:, :E], pre[:, E : 2 * E], pre[:, 2 * E :]
    exp_q, exp_k = jnp.exp(jnp.minimum(uq, 0.0)), jnp.exp(jnp.minimum(uk, 0.0))
    q = jnp.where(uq > 0, uq + 1.0, exp_q)
    kf = jnp.where(uk > 0, uk + 1.0, exp_k)
    slope_q = jnp.where(uq > 0, 1.0, exp_q)
    slope_k = jnp.where(uk > 0, 1.0, exp_k)
    qb, kb, vb = q.astype(BF16), kf.astype(BF16), v.astype(BF16)

    sts[...] = nn(jnp.transpose(kf).astype(BF16), vb).astype(BF16)
    for k in range(1, NZ):
        @pl.when(s + k < NZ)
        def _():
            copy(sts, str_.at[k - 1], st_s.at[k - 1], st_r.at[k - 1], at_seq(k)).start()

    rows = lax.broadcasted_iota(jnp.int32, (TB, TB), 0)
    cols = lax.broadcasted_iota(jnp.int32, (TB, TB), 1)
    sc[...] = jnp.where(rows >= cols, nt(qb, kb), 0.0).astype(BF16)
    sct[...] = jnp.where(rows <= cols, nt(kb, qb), 0.0).astype(BF16)
    nu[...] = nn(sc[...], vb)
    inc[...] = jnp.zeros_like(inc)
    for k in range(1, NZ):
        @pl.when(s >= k)
        def _():
            arrived(str_.at[k - 1], st_s.at[k - 1], st_r.at[k - 1])
            inc[...] += str_[k - 1].astype(F32)

    inb = inc[...].astype(BF16)
    num = nu[...] + nn(qb, inb)
    inv = lax.rsqrt(jnp.mean(num * num, axis=-1, keepdims=True) + EPSILON)
    normed = num * inv
    att_out[...] = normed.astype(BF16)
    up = gout[...].astype(F32)
    dn = inv * (up - normed * jnp.mean(up * normed, axis=-1, keepdims=True))
    dnb = dn.astype(BF16)
    sus[...] = nn(jnp.transpose(q).astype(BF16), dnb).astype(BF16)
    for k in range(1, NZ):
        @pl.when(s >= k)
        def _():
            copy(sus, sur.at[k - 1], su_s.at[k - 1], su_r.at[k - 1], at_seq(NZ - k)).start()

    ds[...] = jnp.where(rows >= cols, nt(dnb, vb), 0.0).astype(BF16)
    dst[...] = jnp.where(rows <= cols, nt(vb, dnb), 0.0).astype(BF16)
    dq = (nn(ds[...], kb) + nt(dnb, inb)) * slope_q
    dki[...] = nn(dst[...], qb)
    dvi[...] = nn(sct[...], dnb)
    suf[...] = jnp.zeros_like(suf)
    for k in range(1, NZ):
        @pl.when(s + k < NZ)
        def _():
            arrived(sur.at[k - 1], su_s.at[k - 1], su_r.at[k - 1])
            suf[...] += sur[k - 1].astype(F32)

    sfb = suf[...].astype(BF16)
    dk = (dki[...] + nt(vb, sfb)) * slope_k
    dv = dvi[...] + nn(kb, sfb)
    grad = jnp.concatenate([dq, dk, dv], axis=1)
    signed = grad * so
    gb[...] = grad.astype(BF16)
    gsb[...] = signed.astype(BF16)
    gt[...] = jnp.transpose(grad).astype(BF16)
    gst[...] = jnp.transpose(signed).astype(BF16)

    def partials(first, stride, count):
        def one(i, carry):
            e = lax.rem(s + first + i * stride, NZ)
            t = columns(ta, e)
            gp[e, 0] = nn(gt[...], t).astype(BF16)
            gp[e, 1] = nn(gst[...], t * columns(sa, e)).astype(BF16)
            return carry

        lax.fori_loop(0, count, one, 0)

    def sum_out(way, left, m):
        e = lax.rem(s + (left if way == 0 else NZ - left), NZ)
        if left < 3 or (left == 3 and m == way):
            arrived(rr.at[way, left, m], rs_s.at[way, left, m], rs_r.at[way, left, m])
            gp[e, m] = (gp[e, m].astype(F32) + rr[way, left, m].astype(F32)).astype(BF16)
        start(
            gp.at[e, m], rr.at[way, left - 1, m], rs_s.at[way, left - 1, m], rs_r.at[way, left - 1, m],
            at_seq(1 if way == 0 else NZ - 1),
        )

    partials(4, 1, 1)
    sum_out(0, 4, 0)
    sum_out(1, 4, 1)
    partials(3, 2, 2)
    sum_out(0, 3, 1)
    sum_out(1, 3, 0)

    def back(e, carry):
        term = nt(gb[...], w_all[e, 0]) + columns(sa, e).astype(F32) * nt(gsb[...], w_all[e, 1])
        term = term.astype(BF16)
        row, first = lax.div(e, 2), 2 * lax.rem(e, 2)
        for j in range(4):
            bp[j % 2, row, first + j // 2] = term[:, j * DB : (j + 1) * DB]
        return carry

    for g in range(4):
        lax.fori_loop(2 * g, 2 * g + 2, back, 0)
        start(bp.at[oc, g], cr.at[g], bc_s.at[g], bc_r.at[g], partner)

    sum_out(0, 3, 0)
    sum_out(1, 3, 1)
    partials(NZ - 2, 1, 5)

    for g in range(4):
        arrived(cr.at[g], bc_s.at[g], bc_r.at[g])

    def join(i, carry):
        a, b = lax.div(i, 4), lax.rem(i, 4)
        bp[c, a, b] = (bp[c, a, b].astype(F32) + cr[a, b].astype(F32)).astype(BF16)
        return carry

    lax.fori_loop(0, 16, join, 0)
    top, low = pl.ds(0, HALF), pl.ds(HALF, HALF)
    for k in (1, 2, 3):
        start(bp.at[c, :, lax.rem(x + k, 4), top], xr.at[k - 1], bx_s.at[k - 1], bx_r.at[k - 1], at_x(k))
        start(bp.at[c, lax.rem(y + k, 4), :, low], yr.at[k - 1], by_s.at[k - 1], by_r.at[k - 1], at_y(k))

    sum_out(0, 2, 1)
    sum_out(1, 2, 0)
    sum_out(0, 2, 0)
    sum_out(1, 2, 1)

    for k in (1, 2, 3):
        arrived(xr.at[k - 1], bx_s.at[k - 1], bx_r.at[k - 1])
        arrived(yr.at[k - 1], by_s.at[k - 1], by_r.at[k - 1])
    for i in range(4):
        total = bp[c, i, x, top].astype(F32)
        other = bp[c, y, i, low].astype(F32)
        for k in range(3):
            total += xr[k, i].astype(F32)
            other += yr[k, i].astype(F32)
        xb[i] = total.astype(BF16)
        yb[i] = other.astype(BF16)
    for k in (1, 2, 3):
        start(xb.at[lax.rem(y + k, 4)], xr2.at[k - 1], by_s.at[2 + k], by_r.at[2 + k], at_y(k))
        start(yb.at[lax.rem(x + k, 4)], yr2.at[k - 1], bx_s.at[2 + k], bx_r.at[2 + k], at_x(k))

    sum_out(0, 1, 1)
    sum_out(1, 1, 0)

    for k in (1, 2, 3):
        arrived(xr2.at[k - 1], by_s.at[2 + k], by_r.at[2 + k])
        arrived(yr2.at[k - 1], bx_s.at[2 + k], bx_r.at[2 + k])
    total = xb[y].astype(F32)
    other = yb[x].astype(F32)
    for k in range(3):
        total += xr2[k].astype(F32)
        other += yr2[k].astype(F32)
    dtok_out[top, :] = total.astype(BF16)
    dtok_out[low, :] = other.astype(BF16)

    sum_out(0, 1, 0)
    sum_out(1, 1, 1)
    for m, out in ((1, gs_out), (0, gm_out)):
        for way in (0, 1):
            arrived(rr.at[way, 0, m], rs_s.at[way, 0, m], rs_r.at[way, 0, m])
        total = gp[s, m].astype(F32) + rr[0, 0, m].astype(F32) + rr[1, 0, m].astype(F32)
        out[...] = jnp.transpose(total).astype(BF16)

    for one in pending:
        one.wait_send()
    for k in range(1, NZ):
        @pl.when(s + k < NZ)
        def _():
            copy(sts, str_.at[k - 1], st_s.at[k - 1], st_r.at[k - 1], at_seq(k)).wait_send()

        @pl.when(s >= k)
        def _():
            copy(sus, sur.at[k - 1], su_s.at[k - 1], su_r.at[k - 1], at_seq(NZ - k)).wait_send()


def local(tokens, in_mask, out_mask, w_mean, w_sigma, grad_out):
    sgn = (2 * out_mask - 1).astype(BF16).reshape(TB, C)
    vm = pltpu.VMEM
    dma = pltpu.SemaphoreType.DMA
    attended, d_tokens, g_mean, g_sigma = pl.pallas_call(
        kernel,
        out_shape=(
            jax.ShapeDtypeStruct((TB, E), BF16),
            jax.ShapeDtypeStruct((TB, DB), BF16),
            jax.ShapeDtypeStruct((KB, C), BF16),
            jax.ShapeDtypeStruct((KB, C), BF16),
        ),
        in_specs=[pl.BlockSpec(memory_space=vm)] * 6,
        out_specs=[pl.BlockSpec(memory_space=vm)] * 4,
        scratch_shapes=[
            vm((2, 4, 4, TB, DB), BF16),
            vm((2, 4, 4, TB, DB), BF16),
            vm((NZ, 2, KB, C), BF16),
            vm((TB, C), F32),
            vm((TB, C), F32),
            vm((E, E), BF16),
            vm((NZ - 1, E, E), BF16),
            vm((E, E), BF16),
            vm((NZ - 1, E, E), BF16),
            vm((E, E), F32),
            vm((E, E), F32),
            vm((TB, TB), BF16),
            vm((TB, TB), BF16),
            vm((TB, TB), BF16),
            vm((TB, TB), BF16),
            vm((TB, E), F32),
            vm((TB, E), F32),
            vm((TB, E), F32),
            vm((TB, C), BF16),
            vm((TB, C), BF16),
            vm((C, TB), BF16),
            vm((C, TB), BF16),
            vm((NZ, 2, C, KB), BF16),
            vm((2, 4, 2, C, KB), BF16),
            vm((2, 4, 4, TB, DB), BF16),
            vm((4, 4, TB, DB), BF16),
            vm((3, 4, HALF, DB), BF16),
            vm((3, 4, HALF, DB), BF16),
            vm((4, HALF, DB), BF16),
            vm((4, HALF, DB), BF16),
            vm((3, HALF, DB), BF16),
            vm((3, HALF, DB), BF16),
            dma((2, 4, 2)), dma((2, 4, 2)),
            dma((6,)), dma((6,)),
            dma((6,)), dma((6,)),
            dma((8,)), dma((8,)),
            dma((7,)), dma((7,)),
            dma((7,)), dma((7,)),
            dma((2, 4, 2)), dma((2, 4, 2)),
            dma((4,)), dma((4,)),
            dma((6,)), dma((6,)),
            dma((6,)), dma((6,)),
        ],
        compiler_params=pltpu.CompilerParams(
            collective_id=0, has_side_effects=True, vmem_limit_bytes=56 * 1024 * 1024
        ),
        name="flipout_layer",
    )(tokens, in_mask, sgn, w_mean.reshape(KB, C), w_sigma.reshape(KB, C), grad_out)
    return attended, d_tokens, g_mean.reshape(KB, 1, C), g_sigma.reshape(KB, 1, C)


def solution(mesh):
    placed = (
        P("seq", "fsdp"),
        P("seq", "fsdp"),
        P("seq", "fsdp", None),
        P("seq", "fsdp", None),
        P("seq", "fsdp", None),
        P("seq", "fsdp"),
    )
    return jax.shard_map(
        local,
        mesh=mesh,
        in_specs=placed,
        out_specs=(P("seq", "fsdp"), P("seq", "fsdp"), P("seq", "fsdp", None), P("seq", "fsdp", None)),
        check_vma=False,
    )
```

time: 581 us -> 158 us (0.27)
  waiting for transfers between devices: 447 us -> 0 us
  Pallas kernels: 0 us -> 150 us
  blocking collectives: 51.3 us -> 0 us
  matrix products: 43.4 us -> 0 us
  local copies, waits for them, and re-layouts: 20.9 us -> 5.07 us
  between operations: 14.3 us -> 0.65 us
    all_gather x4 -> x0, waiting for transfers between devices: 195 us -> none  [the longest x1 54.6 us: local(): lax.all_gather(flipped, 'fsdp', axis=1, tiled=True)]
    unnamed x10 -> x0, waiting for transfers between devices: 157 us -> none
    pallas_call x0 -> x1, Pallas kernels: none -> 150 us  [local(): pl.pallas_call(kernel, out_shape=(jax.ShapeDtypeStruct((TB, E), BF16), ja...]
    reduce_scatter x2 -> x0, waiting for transfers between devices: 94.8 us -> none  [the longest x1 47.9 us: local(): lax.psum_scatter(part_mean.astype(jnp.bfloat16), 'seq', scatter_dimension...]
    all_gather x2 -> x0, blocking collectives: 51.3 us -> none  [the longest x1 26.3 us: prefix(): gathered = lax.all_gather(shard.astype(jnp.bfloat16), axis)]
    dot_general x18 -> x0, matrix products: 43.4 us -> none  [the longest x1 6.43 us: local(): jnp.einsum('td,thc->dhc', gathered_flip, grad_sigma, preferred_element_ty...]
    unnamed x10 -> x8, local copies, waits for them, and re-layouts: 20.9 us -> 5.07 us
  transfers between devices with their start and end apart: 8 -> 0, of which waited for: 8 -> 0; matrix products, arithmetic and copies ran while one was open for 7% -> 0% of each run, Pallas kernels for 0% -> 0%
where the time goes in v1:
time: 158 us
  Pallas kernels  150 us (95%)
  local copies, waits for them, and re-layouts  5.07 us (3%)
  other arithmetic  1.98 us (1%)
    pallas_call x1, Pallas kernels, local(): pl.pallas_call(kernel, out_shape=(jax.ShapeDtypeStruct((TB, E), BF16), ja...  150 us
    unnamed x8, local copies, waits for them, and re-layouts  5.07 us

profile of v1, /device:TPU:4, one launch (start us, length us, event | category | flops | bytes accessed | tf_op | source)
XLA Modules:
  0.0 157.8 jit_solution(14740580033999400312)
XLA Ops:
  0.6 2.0 %fusion.2.sgn = bf16[512,384]{1,0:T(8,128)(2,1)} fusion(s32[512,1,384]{2,1,0:T(1,128)} %param.8), kind=kLoop, calls=%fused_computation.3 | loop fusion | flops 589824 | bytes 1179648 | tf_op jit(solution)/shard_map/reshape | solution.py:329
  2.6 150.1 %flipout_layer.1 = (bf16[512,128]{1,0:T(8,128)(2,1)}, bf16[512,128]{1,0:T(8,128)(2,1)}, bf16[512,384]{1,0:T(8,128)(2,1)}, bf16[512,384]{1,0:T(8,128)(2,1)}) custom-call(bf16[512,128]{1,0:T(8,128)(2,1)} %tok.1, s32[512,128]{1,0:T(8,128)} %in_mask.1, bf16[512,384]{1,0:T(8,128)(2,1)} %fusion.2.sgn, bf16[512,384]{1,0:T(8,128)(2,1)} %bitcast.8, ...), custom_call_target="tpu_custom_call" | custom-call | tf_op jit(solution)/shard_map/flipout_layer/pallas_call | solution.py:332
  152.8 0.0 copy-start.1
  152.8 1.6 %copy.22 = bf16[512,128]{1,0:T(8,128)(2,1)} copy(bf16[512,128]{1,0:T(8,128)(2,1)} %get-tuple-element.16) | data formatting | bytes 262144
  154.4 1.6 copy.23
  156.0 0.0 copy-done.1
  156.0 0.0 copy-start
  156.0 0.7 copy.24
  156.7 0.4 copy-done
  157.1 0.7 copy.25
Async XLA Ops:
  152.8 3.2 %copy-start.1 = (bf16[512,384]{1,0:T(8,128)(2,1)S(1)}, bf16[512,384]{1,0:T(8,128)(2,1)}, u32[]{:S(2)}) copy-start(bf16[512,384]{1,0:T(8,128)(2,1)} %get-tuple-element.10) | copy-start | bytes 1179652
  156.0 1.1 copy-start

commit v2 on v1

--- a/solution.py
+++ b/solution.py
@@ -16,6 +16,7 @@
 C = 3 * E
 NZ = 8
 HALF = TB // 2
+Q = TB // 4
 
 
 def nn(a, b):
@@ -27,11 +28,11 @@
 
 
 def kernel(
-    tok, in_mask, sgn, w_mean, w_sigma, gout,
+    tok, in_mask, out_mask, w_mean, w_sigma, gout,
     att_out, dtok_out, gm_out, gs_out,
-    ta, sa, w_all, pm, ps, sts, str_, sus, sur, inc, suf, sc, sct, ds, dst, nu, dki, dvi,
-    gb, gsb, gt, gst, gp, rr, bp, cr, xr, yr, xb, yb, xr2, yr2,
-    zs, zr, ts, tr, ss, sr, cs, crs, st_s, st_r, su_s, su_r, rs_s, rs_r, bc_s, bc_r, bx_s, bx_r, by_s, by_r,
+    ta, sa, sgn, w_all, pm, ps, sts, str_, sus, sur, inc, suf, sc, sct, ds, dst, nu, dki, dvi,
+    gb, gsb, tq, t2, s2, so_all, gt_all, gmt, gst, bp, cr, xr, yr, xb, yb, xr2, yr2,
+    zs, zr, ts, tr, ss, sr, cs, crs, st_s, st_r, su_s, su_r, q_s, q_r, z2_s, z2_r, t3_s, t3_r, s3_s, s3_r, c3_s, c3_r, so_s, so_r, g_s, g_r, bc_s, bc_r, bx_s, bx_r, by_s, by_r,
 ):
     s = lax.axis_index("seq")
     f = lax.axis_index("fsdp")
@@ -49,6 +50,12 @@
     def at_y(k):
         return (s, (lax.rem(y + k, 4) * 4 + x) * 2 + c)
 
+    def quarter(row):
+        return pl.ds(pl.multiple_of(row * Q, Q), Q)
+
+    side = lax.rem(x, 2)
+    odd = lax.div(x, 2)
+    holder = odd == lax.rem(s, 2)
     partner = (s, (y * 4 + x) * 2 + oc)
     pending = []
 
@@ -71,6 +78,7 @@
         pl.semaphore_signal(barrier, inc=1, device_id=peer, device_id_type=MESH)
 
     ta[c, y, x] = tok[...]
+    tq[y] = tok[quarter(y), :]
     sa[c, y, x] = (2 * in_mask[...] - 1).astype(F32).astype(BF16)
     w_all[s, 0] = w_mean[...]
     w_all[s, 1] = w_sigma[...]
@@ -96,9 +104,31 @@
         ring_out(0, 0, part)
         ring_out(1, 0, 1 - part)
 
+    def ring(ref_all, send, recv):
+        def part(owner, way, hop):
+            return ref_all.at[owner] if hop < 3 else ref_all.at[owner, pl.ds(way * (C // 2), C // 2)]
+
+        def out(hop):
+            for way in (0, 1):
+                ref = part(lax.rem(s + (NZ - hop if way == 0 else hop), NZ), way, hop)
+                start(ref, ref, send.at[way, hop], recv.at[way, hop], at_seq(1 if way == 0 else NZ - 1))
+
+        def step(hop):
+            for way in (0, 1):
+                owner = lax.rem(s + (NZ - 1 - hop if way == 0 else 1 + hop), NZ)
+                arrived(part(owner, way, hop), send.at[way, hop], recv.at[way, hop])
+            if hop < 3:
+                out(hop + 1)
+
+        return out, step
+
+    so_out, so_step = ring(so_all, so_s, so_r)
+    g_out, g_step = ring(gt_all, g_s, g_r)
+
     for k in (1, 2, 3):
         start(ta.at[c, y, x], ta.at[c, y, x], ts.at[k - 1], tr.at[k - 1], at_x(k))
         start(sa.at[c, y, x], sa.at[c, y, x], ss.at[k - 1], sr.at[k - 1], at_y(k))
+        start(ta.at[c, y, x, quarter(lax.rem(y + k, 4))], tq.at[y], q_s.at[k - 1], q_r.at[k - 1], at_y(k))
     for k in (1, 2, 3):
         arrived(ta.at[c, y, lax.rem(x + 4 - k, 4)], ts.at[k - 1], tr.at[k - 1])
     for k in (1, 2, 3):
@@ -110,6 +140,42 @@
     start(ta.at[c, y], ta.at[c, y], cs.at[0], crs.at[0], partner)
     start(sa.at[c, :, x], sa.at[c, :, x], cs.at[4], crs.at[4], partner)
 
+    for k in (1, 2, 3):
+        arrived(tq.at[lax.rem(y + 4 - k, 4)], q_s.at[k - 1], q_r.at[k - 1])
+
+    def to_planes(act):
+        for row in range(4):
+            plane = 2 * row + odd
+
+            @pl.when(plane != s)
+            def _():
+                act(copy(tq.at[row], t2.at[c, y, side, s], z2_s.at[0, row], z2_r.at[0, s], (plane, f)))
+                act(copy(sa.at[c, row, x, quarter(y)], s2.at[c, y, side, s], z2_s.at[1, row], z2_r.at[1, s], (plane, f)))
+
+    to_planes(lambda one: one.start())
+
+    @pl.when(holder)
+    def _():
+        t2[c, y, side, s] = tq[lax.div(s, 2)]
+        s2[c, y, side, s] = sa[c, lax.div(s, 2), x, quarter(y), :]
+
+    def spread_first(act):
+        for k in (1, 2, 3):
+            act(copy(t2.at[c, y, side], t2.at[c, y, side], t3_s.at[k - 1], t3_r.at[side], at_x(k)))
+            act(copy(s2.at[c, y, side], s2.at[c, y, side], s3_s.at[k - 1], s3_r.at[k - 1], at_y(k)))
+
+    def spread_signs(act):
+        for k in (1, 2, 3):
+            act(copy(s2.at[c, :, side], s2.at[c, :, side], s3_s.at[2 + k], s3_r.at[3 + side], at_x(k)))
+
+    def from_holders(ref_of, send, recv):
+        for b in (0, 1):
+            @pl.when(2 * lax.rem(s, 2) + b != x)
+            def _():
+                arrived(ref_of(b), send, recv(b))
+
+    sgn[...] = (2 * out_mask[:, 0, :] - 1).astype(F32)
+    so_all[s] = jnp.transpose(sgn[...]).astype(BF16)
     ring_step(0, 0)
     ring_step(0, 1)
     ring_step(1, 0)
@@ -120,6 +186,14 @@
         xk = lax.rem(x + 4 - k, 4)
         arrived(sa.at[c, :, xk], ss.at[2 + k], sr.at[2 + k])
         start(sa.at[c, :, xk], sa.at[c, :, xk], cs.at[4 + k], crs.at[4 + k], partner)
+    @pl.when(holder)
+    def _():
+        for k in range(1, NZ):
+            source = lax.rem(s + k, NZ)
+            arrived(t2.at[c, y, side, source], z2_s.at[0, 0], z2_r.at[0, source])
+            arrived(s2.at[c, y, side, source], z2_s.at[1, 0], z2_r.at[1, source])
+        spread_first(lambda one: one.start())
+
     ring_step(1, 1)
     for k in range(4):
         arrived(ta.at[oc, lax.rem(y + 4 - k, 4)], cs.at[k], crs.at[k])
@@ -144,13 +218,24 @@
 
     project(NZ - 2, 1, 5)
     ring_step(2, 0)
+    from_holders(lambda b: t2.at[c, y, b], t3_s.at[0], lambda b: t3_r.at[b])
+    for k in (1, 2, 3):
+        start(t2.at[c, y], t2.at[c, y], t3_s.at[2 + k], t3_r.at[1 + k], at_y(k))
+
+    @pl.when(holder)
+    def _():
+        for k in (1, 2, 3):
+            arrived(s2.at[c, lax.rem(y + 4 - k, 4), side], s3_s.at[k - 1], s3_r.at[k - 1])
+        spread_signs(lambda one: one.start())
+
     ring_step(2, 1)
     project(NZ - 3, 6, 2)
     ring_in(0, 3, 0)
     ring_in(1, 3, 1)
+    so_out(0)
     project(4, 1, 1)
 
-    so = sgn[...].astype(F32)
+    so = sgn[...]
     pre = pm[...] + ps[...] * so
     uq, uk, v = pre[:, :E], pre[:, E : 2 * E], pre[:, 2 * E :]
     exp_q, exp_k = jnp.exp(jnp.minimum(uq, 0.0)), jnp.exp(jnp.minimum(uk, 0.0))
@@ -172,6 +257,13 @@
     sct[...] = jnp.where(rows <= cols, nt(kb, qb), 0.0).astype(BF16)
     nu[...] = nn(sc[...], vb)
     inc[...] = jnp.zeros_like(inc)
+    for k in (1, 2, 3):
+        arrived(t2.at[c, lax.rem(y + 4 - k, 4)], t3_s.at[2 + k], t3_r.at[1 + k])
+    from_holders(lambda b: s2.at[c, :, b], s3_s.at[3], lambda b: s3_r.at[3 + b])
+    for k in range(4):
+        start(t2.at[c, k], t2.at[c, k], c3_s.at[k], c3_r.at[k], partner)
+    for b in range(2):
+        start(s2.at[c, :, b], s2.at[c, :, b], c3_s.at[4 + b], c3_r.at[4 + b], partner)
     for k in range(1, NZ):
         @pl.when(s >= k)
         def _():
@@ -198,6 +290,7 @@
     dki[...] = nn(dst[...], qb)
     dvi[...] = nn(sct[...], dnb)
     suf[...] = jnp.zeros_like(suf)
+    so_step(0)
     for k in range(1, NZ):
         @pl.when(s + k < NZ)
         def _():
@@ -209,37 +302,27 @@
     dv = dvi[...] + nn(kb, sfb)
     grad = jnp.concatenate([dq, dk, dv], axis=1)
     signed = grad * so
+    gt_all[s] = jnp.transpose(grad).astype(BF16)
+    g_out(0)
     gb[...] = grad.astype(BF16)
     gsb[...] = signed.astype(BF16)
-    gt[...] = jnp.transpose(grad).astype(BF16)
-    gst[...] = jnp.transpose(signed).astype(BF16)
-
-    def partials(first, stride, count):
+    so_step(1)
+
+    gmt[...] = jnp.zeros_like(gmt)
+    gst[...] = jnp.zeros_like(gst)
+
+    def block(ref, owner):
+        return jnp.concatenate([ref[j % 2, :, j // 2, owner].reshape(TB, DB) for j in range(4)], axis=1)
+
+    def gather_grads(first, stride, count):
         def one(i, carry):
-            e = lax.rem(s + first + i * stride, NZ)
-            t = columns(ta, e)
-            gp[e, 0] = nn(gt[...], t).astype(BF16)
-            gp[e, 1] = nn(gst[...], t * columns(sa, e)).astype(BF16)
+            owner = lax.rem(s + first + i * stride, NZ)
+            t, g = block(t2, owner), gt_all[owner]
+            gmt[...] += nn(g, t)
+            gst[...] += nn(g * so_all[owner], t * block(s2, owner))
             return carry
 
         lax.fori_loop(0, count, one, 0)
-
-    def sum_out(way, left, m):
-        e = lax.rem(s + (left if way == 0 else NZ - left), NZ)
-        if left < 3 or (left == 3 and m == way):
-            arrived(rr.at[way, left, m], rs_s.at[way, left, m], rs_r.at[way, left, m])
-            gp[e, m] = (gp[e, m].astype(F32) + rr[way, left, m].astype(F32)).astype(BF16)
-        start(
-            gp.at[e, m], rr.at[way, left - 1, m], rs_s.at[way, left - 1, m], rs_r.at[way, left - 1, m],
-            at_seq(1 if way == 0 else NZ - 1),
-        )
-
-    partials(4, 1, 1)
-    sum_out(0, 4, 0)
-    sum_out(1, 4, 1)
-    partials(3, 2, 2)
-    sum_out(0, 3, 1)
-    sum_out(1, 3, 0)
 
     def back(e, carry):
         term = nt(gb[...], w_all[e, 0]) + columns(sa, e).astype(F32) * nt(gsb[...], w_all[e, 1])
@@ -253,9 +336,13 @@
         lax.fori_loop(2 * g, 2 * g + 2, back, 0)
         start(bp.at[oc, g], cr.at[g], bc_s.at[g], bc_r.at[g], partner)
 
-    sum_out(0, 3, 0)
-    sum_out(1, 3, 1)
-    partials(NZ - 2, 1, 5)
+    for k in range(4):
+        arrived(t2.at[oc, k], c3_s.at[k], c3_r.at[k])
+    for b in range(2):
+        arrived(s2.at[oc, :, b], c3_s.at[4 + b], c3_r.at[4 + b])
+    gather_grads(0, 1, 1)
+    g_step(0)
+    so_step(2)
 
     for g in range(4):
         arrived(cr.at[g], bc_s.at[g], bc_r.at[g])
@@ -271,10 +358,8 @@
         start(bp.at[c, :, lax.rem(x + k, 4), top], xr.at[k - 1], bx_s.at[k - 1], bx_r.at[k - 1], at_x(k))
         start(bp.at[c, lax.rem(y + k, 4), :, low], yr.at[k - 1], by_s.at[k - 1], by_r.at[k - 1], at_y(k))
 
-    sum_out(0, 2, 1)
-    sum_out(1, 2, 0)
-    sum_out(0, 2, 0)
-    sum_out(1, 2, 1)
+    gather_grads(1, 6, 2)
+    g_step(1)
 
     for k in (1, 2, 3):
         arrived(xr.at[k - 1], bx_s.at[k - 1], bx_r.at[k - 1])
@@ -291,8 +376,9 @@
         start(xb.at[lax.rem(y + k, 4)], xr2.at[k - 1], by_s.at[2 + k], by_r.at[2 + k], at_y(k))
         start(yb.at[lax.rem(x + k, 4)], yr2.at[k - 1], bx_s.at[2 + k], bx_r.at[2 + k], at_x(k))
 
-    sum_out(0, 1, 1)
-    sum_out(1, 1, 0)
+    gather_grads(2, 4, 2)
+    g_step(2)
+    so_step(3)
 
     for k in (1, 2, 3):
         arrived(xr2.at[k - 1], by_s.at[2 + k], by_r.at[2 + k])
@@ -305,13 +391,18 @@
     dtok_out[top, :] = total.astype(BF16)
     dtok_out[low, :] = other.astype(BF16)
 
-    sum_out(0, 1, 0)
-    sum_out(1, 1, 1)
-    for m, out in ((1, gs_out), (0, gm_out)):
-        for way in (0, 1):
-            arrived(rr.at[way, 0, m], rs_s.at[way, 0, m], rs_r.at[way, 0, m])
-        total = gp[s, m].astype(F32) + rr[0, 0, m].astype(F32) + rr[1, 0, m].astype(F32)
-        out[...] = jnp.transpose(total).astype(BF16)
+    gather_grads(3, 2, 2)
+    g_step(3)
+    gather_grads(4, 1, 1)
+    gm_out[...] = jnp.transpose(gmt[...]).astype(BF16)
+    gs_out[...] = jnp.transpose(gst[...]).astype(BF16)
+
+    to_planes(lambda one: one.wait_send())
+
+    @pl.when(holder)
+    def _():
+        spread_first(lambda one: one.wait_send())
+        spread_signs(lambda one: one.wait_send())
 
     for one in pending:
         one.wait_send()
@@ -325,11 +416,19 @@
             copy(sus, sur.at[k - 1], su_s.at[k - 1], su_r.at[k - 1], at_seq(NZ - k)).wait_send()
 
 
+def hand_over(*refs):
+    n = len(refs) // 2
+    copies = [pltpu.make_async_copy(refs[i], refs[n + i], refs[2 * n].at[i]) for i in range(n)]
+    for one in copies:
+        one.start()
+    for one in copies:
+        one.wait()
+
+
 def local(tokens, in_mask, out_mask, w_mean, w_sigma, grad_out):
-    sgn = (2 * out_mask - 1).astype(BF16).reshape(TB, C)
     vm = pltpu.VMEM
     dma = pltpu.SemaphoreType.DMA
-    attended, d_tokens, g_mean, g_sigma = pl.pallas_call(
+    results = pl.pallas_call(
         kernel,
         out_shape=(
             jax.ShapeDtypeStruct((TB, E), BF16),
@@ -342,6 +441,7 @@
         scratch_shapes=[
             vm((2, 4, 4, TB, DB), BF16),
             vm((2, 4, 4, TB, DB), BF16),
+            vm((TB, C), F32),
             vm((NZ, 2, KB, C), BF16),
             vm((TB, C), F32),
             vm((TB, C), F32),
@@ -360,10 +460,13 @@
             vm((TB, E), F32),
             vm((TB, C), BF16),
             vm((TB, C), BF16),
-            vm((C, TB), BF16),
-            vm((C, TB), BF16),
-            vm((NZ, 2, C, KB), BF16),
-            vm((2, 4, 2, C, KB), BF16),
+            vm((4, Q, DB), BF16),
+            vm((2, 4, 2, NZ, Q, DB), BF16),
+            vm((2, 4, 2, NZ, Q, DB), BF16),
+            vm((NZ, C, TB), BF16),
+            vm((NZ, C, TB), BF16),
+            vm((C, KB), F32),
+            vm((C, KB), F32),
             vm((2, 4, 4, TB, DB), BF16),
             vm((4, 4, TB, DB), BF16),
             vm((3, 4, HALF, DB), BF16),
@@ -378,7 +481,13 @@
             dma((8,)), dma((8,)),
             dma((7,)), dma((7,)),
             dma((7,)), dma((7,)),
-            dma((2, 4, 2)), dma((2, 4, 2)),
+            dma((3,)), dma((3,)),
+            dma((2, 4)), dma((2, NZ)),
+            dma((6,)), dma((5,)),
+            dma((6,)), dma((5,)),
+            dma((6,)), dma((6,)),
+            dma((2, 4)), dma((2, 4)),
+            dma((2, 4)), dma((2, 4)),
             dma((4,)), dma((4,)),
             dma((6,)), dma((6,)),
             dma((6,)), dma((6,)),
@@ -387,7 +496,15 @@
             collective_id=0, has_side_effects=True, vmem_limit_bytes=56 * 1024 * 1024
         ),
         name="flipout_layer",
-    )(tokens, in_mask, sgn, w_mean.reshape(KB, C), w_sigma.reshape(KB, C), grad_out)
+    )(tokens, in_mask, out_mask, w_mean.reshape(KB, C), w_sigma.reshape(KB, C), grad_out)
+    attended, d_tokens, g_mean, g_sigma = pl.pallas_call(
+        hand_over,
+        out_shape=[jax.ShapeDtypeStruct(r.shape, r.dtype) for r in results],
+        in_specs=[pl.BlockSpec(memory_space=pl.ANY)] * 4,
+        out_specs=[pl.BlockSpec(memory_space=vm)] * 4,
+        scratch_shapes=[dma((4,))],
+        name="hand_over",
+    )(*results)
     return attended, d_tokens, g_mean.reshape(KB, 1, C), g_sigma.reshape(KB, 1, C)
 
 

time: 158 us -> 173 us (1.095); the launches traced: 158 us -> 170 us
  Pallas kernels: 150 us -> 170 us
  local copies, waits for them, and re-layouts: 5.07 us -> 0 us
  other arithmetic: 1.98 us -> 0 us
    pallas_call x1, Pallas kernels: 150 us -> 167 us  [local(): pl.pallas_call(kernel, out_shape=(jax.ShapeDtypeStruct((TB, E), BF16), ja...]
    unnamed x8 -> x0, local copies, waits for them, and re-layouts: 5.07 us -> none
    pallas_call x0 -> x1, Pallas kernels: none -> 2.25 us  [local(): pl.pallas_call(hand_over, out_shape=[jax.ShapeDtypeStruct(r.shape, r.dtyp...]
    reshape x1 -> x0, other arithmetic: 1.98 us -> none  [local(): sgn = (2 * out_mask - 1).astype(BF16).reshape(TB, C)]
where the time goes in v2:
time: 173 us; the launch traced here: 170 us
  Pallas kernels  170 us (98%)
    pallas_call x1, Pallas kernels, local(): pl.pallas_call(kernel, out_shape=(jax.ShapeDtypeStruct((TB, E), BF16), ja...  167 us

profile of v2, /device:TPU:4, one launch (start us, length us, event | category | flops | bytes accessed | tf_op | source)
XLA Modules:
  0.0 170.2 jit_solution(5236021064658375499)
XLA Ops:
  0.6 167.3 %flipout_layer.1 = (bf16[512,128]{1,0:T(8,128)(2,1)}, bf16[512,128]{1,0:T(8,128)(2,1)}, bf16[512,384]{1,0:T(8,128)(2,1)}, bf16[512,384]{1,0:T(8,128)(2,1)}) custom-call(bf16[512,128]{1,0:T(8,128)(2,1)} %tok.1, s32[512,128]{1,0:T(8,128)} %in_mask.1, s32[512,1,384]{2,1,0:T(1,128)} %out_mask.1, bf16[512,384]{1,0:T(8,128)(2,1)} %bitcast.4, ...), custom_call_target="tpu_custom_call" | custom-call | tf_op jit(solution)/shard_map/flipout_layer/pallas_call | solution.py:431
  167.9 2.2 %hand_over.1 = (bf16[512,128]{1,0:T(8,128)(2,1)}, bf16[512,128]{1,0:T(8,128)(2,1)}, bf16[512,384]{1,0:T(8,128)(2,1)}, bf16[512,384]{1,0:T(8,128)(2,1)}) custom-call(bf16[512,128]{1,0:T(8,128)(2,1)} %get-tuple-element.12.refs_0_, bf16[512,128]{1,0:T(8,128)(2,1)} %get-tuple-element.13.refs_1_, bf16[512,384]{1,0:T(8,128)(2,1)} %get-tuple-element.14.refs_2_, ...), custom_call_target="tpu_custom_call" | custom-call | tf_op jit(solution)/shard_map/hand_over/pallas_call | solution.py:500

commit v3 on v1

--- a/solution.py
+++ b/solution.py
@@ -27,9 +27,9 @@
 
 
 def kernel(
-    tok, in_mask, sgn, w_mean, w_sigma, gout,
+    tok, in_mask, out_mask, w_mean, w_sigma, gout,
     att_out, dtok_out, gm_out, gs_out,
-    ta, sa, w_all, pm, ps, sts, str_, sus, sur, inc, suf, sc, sct, ds, dst, nu, dki, dvi,
+    ta, sa, sgn, w_all, pm, ps, sts, str_, sus, sur, inc, suf, sc, sct, ds, dst, nu, dki, dvi,
     gb, gsb, gt, gst, gp, rr, bp, cr, xr, yr, xb, yb, xr2, yr2,
     zs, zr, ts, tr, ss, sr, cs, crs, st_s, st_r, su_s, su_r, rs_s, rs_r, bc_s, bc_r, bx_s, bx_r, by_s, by_r,
 ):
@@ -110,6 +110,7 @@
     start(ta.at[c, y], ta.at[c, y], cs.at[0], crs.at[0], partner)
     start(sa.at[c, :, x], sa.at[c, :, x], cs.at[4], crs.at[4], partner)
 
+    sgn[...] = (2 * out_mask[:, 0, :] - 1).astype(F32)
     ring_step(0, 0)
     ring_step(0, 1)
     ring_step(1, 0)
@@ -150,7 +151,7 @@
     ring_in(1, 3, 1)
     project(4, 1, 1)
 
-    so = sgn[...].astype(F32)
+    so = sgn[...]
     pre = pm[...] + ps[...] * so
     uq, uk, v = pre[:, :E], pre[:, E : 2 * E], pre[:, 2 * E :]
     exp_q, exp_k = jnp.exp(jnp.minimum(uq, 0.0)), jnp.exp(jnp.minimum(uk, 0.0))
@@ -325,11 +326,19 @@
             copy(sus, sur.at[k - 1], su_s.at[k - 1], su_r.at[k - 1], at_seq(NZ - k)).wait_send()
 
 
+def hand_over(*refs):
+    n = len(refs) // 2
+    copies = [pltpu.make_async_copy(refs[i], refs[n + i], refs[2 * n].at[i]) for i in range(n)]
+    for one in copies:
+        one.start()
+    for one in copies:
+        one.wait()
+
+
 def local(tokens, in_mask, out_mask, w_mean, w_sigma, grad_out):
-    sgn = (2 * out_mask - 1).astype(BF16).reshape(TB, C)
     vm = pltpu.VMEM
     dma = pltpu.SemaphoreType.DMA
-    attended, d_tokens, g_mean, g_sigma = pl.pallas_call(
+    results = pl.pallas_call(
         kernel,
         out_shape=(
             jax.ShapeDtypeStruct((TB, E), BF16),
@@ -342,6 +351,7 @@
         scratch_shapes=[
             vm((2, 4, 4, TB, DB), BF16),
             vm((2, 4, 4, TB, DB), BF16),
+            vm((TB, C), F32),
             vm((NZ, 2, KB, C), BF16),
             vm((TB, C), F32),
             vm((TB, C), F32),
@@ -387,7 +397,15 @@
             collective_id=0, has_side_effects=True, vmem_limit_bytes=56 * 1024 * 1024
         ),
         name="flipout_layer",
-    )(tokens, in_mask, sgn, w_mean.reshape(KB, C), w_sigma.reshape(KB, C), grad_out)
+    )(tokens, in_mask, out_mask, w_mean.reshape(KB, C), w_sigma.reshape(KB, C), grad_out)
+    attended, d_tokens, g_mean, g_sigma = pl.pallas_call(
+        hand_over,
+        out_shape=[jax.ShapeDtypeStruct(r.shape, r.dtype) for r in results],
+        in_specs=[pl.BlockSpec(memory_space=pl.ANY)] * 4,
+        out_specs=[pl.BlockSpec(memory_space=vm)] * 4,
+        scratch_shapes=[dma((4,))],
+        name="hand_over",
+    )(*results)
     return attended, d_tokens, g_mean.reshape(KB, 1, C), g_sigma.reshape(KB, 1, C)
 
 

time: 158 us -> 153 us (0.968)
  local copies, waits for them, and re-layouts: 5.07 us -> 0 us
  Pallas kernels: 150 us -> 152 us
  other arithmetic: 1.98 us -> 0 us
    unnamed x8 -> x0, local copies, waits for them, and re-layouts: 5.07 us -> none
    pallas_call x0 -> x1, Pallas kernels: none -> 2.25 us  [local(): pl.pallas_call(hand_over, out_shape=[jax.ShapeDtypeStruct(r.shape, r.dtyp...]
    reshape x1 -> x0, other arithmetic: 1.98 us -> none  [local(): sgn = (2 * out_mask - 1).astype(BF16).reshape(TB, C)]
where the time goes in v3:
time: 153 us
  Pallas kernels  152 us (99%)
    pallas_call x1, Pallas kernels, local(): pl.pallas_call(kernel, out_shape=(jax.ShapeDtypeStruct((TB, E), BF16), ja...  150 us

profile of v3, /device:TPU:4, one launch (start us, length us, event | category | flops | bytes accessed | tf_op | source)
XLA Modules:
  0.0 153.1 jit_solution(7200974038463577664)
XLA Ops:
  0.6 150.2 %flipout_layer.1 = (bf16[512,128]{1,0:T(8,128)(2,1)}, bf16[512,128]{1,0:T(8,128)(2,1)}, bf16[512,384]{1,0:T(8,128)(2,1)}, bf16[512,384]{1,0:T(8,128)(2,1)}) custom-call(bf16[512,128]{1,0:T(8,128)(2,1)} %tok.1, s32[512,128]{1,0:T(8,128)} %in_mask.1, s32[512,1,384]{2,1,0:T(1,128)} %out_mask.1, bf16[512,384]{1,0:T(8,128)(2,1)} %bitcast.4, ...), custom_call_target="tpu_custom_call" | custom-call | tf_op jit(solution)/shard_map/flipout_layer/pallas_call | solution.py:341
  150.9 2.2 %hand_over.1 = (bf16[512,128]{1,0:T(8,128)(2,1)}, bf16[512,128]{1,0:T(8,128)(2,1)}, bf16[512,384]{1,0:T(8,128)(2,1)}, bf16[512,384]{1,0:T(8,128)(2,1)}) custom-call(bf16[512,128]{1,0:T(8,128)(2,1)} %get-tuple-element.12.refs_0_, bf16[512,128]{1,0:T(8,128)(2,1)} %get-tuple-element.13.refs_1_, bf16[512,384]{1,0:T(8,128)(2,1)} %get-tuple-element.14.refs_2_, ...), custom_call_target="tpu_custom_call" | custom-call | tf_op jit(solution)/shard_map/hand_over/pallas_call | solution.py:401

commit v4 on v3

--- a/solution.py
+++ b/solution.py
@@ -31,7 +31,7 @@
     att_out, dtok_out, gm_out, gs_out,
     ta, sa, sgn, w_all, pm, ps, sts, str_, sus, sur, inc, suf, sc, sct, ds, dst, nu, dki, dvi,
     gb, gsb, gt, gst, gp, rr, bp, cr, xr, yr, xb, yb, xr2, yr2,
-    zs, zr, ts, tr, ss, sr, cs, crs, st_s, st_r, su_s, su_r, rs_s, rs_r, bc_s, bc_r, bx_s, bx_r, by_s, by_r,
+    zs, zr, ts, tr, ss, sr, cs, crs, st_s, st_r, su_s, su_r, rs_s, rs_r, eq_s, eq_r, bc_s, bc_r, bx_s, bx_r, by_s, by_r,
 ):
     s = lax.axis_index("seq")
     f = lax.axis_index("fsdp")
@@ -193,9 +193,51 @@
         def _():
             copy(sus, sur.at[k - 1], su_s.at[k - 1], su_r.at[k - 1], at_seq(NZ - k)).start()
 
+    every, query, rest = pl.ds(0, C), pl.ds(0, E), pl.ds(E, C - E)
+
+    def partials(first, stride, count, part):
+        def one(i, carry):
+            e = lax.rem(s + first + i * stride, NZ)
+            t = columns(ta, e)
+            gp[e, 0, part] = nn(gt[part, :], t).astype(BF16)
+            gp[e, 1, part] = nn(gst[part, :], t * columns(sa, e)).astype(BF16)
+            return carry
+
+        lax.fori_loop(0, count, one, 0)
+
+    def in_two(way, left, m):
+        return left == 4 or (left == 3 and m != way)
+
+    def send_sum(way, left, m, part, send, recv):
+        e = lax.rem(s + (left if way == 0 else NZ - left), NZ)
+        start(gp.at[e, m, part], rr.at[way, left - 1, m, part], send, recv, at_seq(1 if way == 0 else NZ - 1))
+
+    def query_out(way, left, m):
+        send_sum(way, left, m, query, eq_s.at[way, left - 3], eq_r.at[way, left - 3])
+
+    def sum_out(way, left, m):
+        e = lax.rem(s + (left if way == 0 else NZ - left), NZ)
+        part = rest if in_two(way, left, m) else every
+        if part is every:
+            if in_two(way, left + 1, m):
+                arrived(rr.at[way, left, m, query], eq_s.at[way, left - 2], eq_r.at[way, left - 2])
+                arrived(rr.at[way, left, m, rest], rs_s.at[way, left, m], rs_r.at[way, left, m])
+            else:
+                arrived(rr.at[way, left, m], rs_s.at[way, left, m], rs_r.at[way, left, m])
+            gp[e, m] = (gp[e, m].astype(F32) + rr[way, left, m].astype(F32)).astype(BF16)
+        send_sum(way, left, m, part, rs_s.at[way, left - 1, m], rs_r.at[way, left - 1, m])
+
     ds[...] = jnp.where(rows >= cols, nt(dnb, vb), 0.0).astype(BF16)
+    dq = (nn(ds[...], kb) + nt(dnb, inb)) * slope_q
+    gt[query, :] = jnp.transpose(dq).astype(BF16)
+    gst[query, :] = jnp.transpose(dq * so[:, :E]).astype(BF16)
+    partials(4, 1, 1, query)
+    query_out(0, 4, 0)
+    query_out(1, 4, 1)
+    partials(3, 2, 2, query)
+    query_out(0, 3, 1)
+    query_out(1, 3, 0)
     dst[...] = jnp.where(rows <= cols, nt(vb, dnb), 0.0).astype(BF16)
-    dq = (nn(ds[...], kb) + nt(dnb, inb)) * slope_q
     dki[...] = nn(dst[...], qb)
     dvi[...] = nn(sct[...], dnb)
     suf[...] = jnp.zeros_like(suf)
@@ -208,39 +250,21 @@
     sfb = suf[...].astype(BF16)
     dk = (dki[...] + nt(vb, sfb)) * slope_k
     dv = dvi[...] + nn(kb, sfb)
-    grad = jnp.concatenate([dq, dk, dv], axis=1)
-    signed = grad * so
-    gb[...] = grad.astype(BF16)
-    gsb[...] = signed.astype(BF16)
-    gt[...] = jnp.transpose(grad).astype(BF16)
-    gst[...] = jnp.transpose(signed).astype(BF16)
-
-    def partials(first, stride, count):
-        def one(i, carry):
-            e = lax.rem(s + first + i * stride, NZ)
-            t = columns(ta, e)
-            gp[e, 0] = nn(gt[...], t).astype(BF16)
-            gp[e, 1] = nn(gst[...], t * columns(sa, e)).astype(BF16)
-            return carry
-
-        lax.fori_loop(0, count, one, 0)
-
-    def sum_out(way, left, m):
-        e = lax.rem(s + (left if way == 0 else NZ - left), NZ)
-        if left < 3 or (left == 3 and m == way):
-            arrived(rr.at[way, left, m], rs_s.at[way, left, m], rs_r.at[way, left, m])
-            gp[e, m] = (gp[e, m].astype(F32) + rr[way, left, m].astype(F32)).astype(BF16)
-        start(
-            gp.at[e, m], rr.at[way, left - 1, m], rs_s.at[way, left - 1, m], rs_r.at[way, left - 1, m],
-            at_seq(1 if way == 0 else NZ - 1),
-        )
-
-    partials(4, 1, 1)
+    later = jnp.concatenate([dk, dv], axis=1)
+    gt[rest, :] = jnp.transpose(later).astype(BF16)
+    gst[rest, :] = jnp.transpose(later * so[:, E:]).astype(BF16)
+
+    partials(4, 1, 1, rest)
     sum_out(0, 4, 0)
     sum_out(1, 4, 1)
-    partials(3, 2, 2)
+    partials(3, 2, 2, rest)
     sum_out(0, 3, 1)
     sum_out(1, 3, 0)
+
+    gb[:, :E] = dq.astype(BF16)
+    gb[:, E:] = later.astype(BF16)
+    gsb[:, :E] = (dq * so[:, :E]).astype(BF16)
+    gsb[:, E:] = (later * so[:, E:]).astype(BF16)
 
     def back(e, carry):
         term = nt(gb[...], w_all[e, 0]) + columns(sa, e).astype(F32) * nt(gsb[...], w_all[e, 1])
@@ -256,7 +280,7 @@
 
     sum_out(0, 3, 0)
     sum_out(1, 3, 1)
-    partials(NZ - 2, 1, 5)
+    partials(NZ - 2, 1, 5, every)
 
     for g in range(4):
         arrived(cr.at[g], bc_s.at[g], bc_r.at[g])
@@ -389,6 +413,7 @@
             dma((7,)), dma((7,)),
             dma((7,)), dma((7,)),
             dma((2, 4, 2)), dma((2, 4, 2)),
+            dma((2, 2)), dma((2, 2)),
             dma((4,)), dma((4,)),
             dma((6,)), dma((6,)),
             dma((6,)), dma((6,)),

time: 153 us -> 151 us (0.987)
  Pallas kernels: 152 us -> 150 us
    pallas_call x1, Pallas kernels: 150 us -> 148 us  [local(): pl.pallas_call(kernel, out_shape=(jax.ShapeDtypeStruct((TB, E), BF16), ja...]
where the time goes in v4:
time: 151 us
  Pallas kernels  150 us (99%)
    pallas_call x1, Pallas kernels, local(): pl.pallas_call(kernel, out_shape=(jax.ShapeDtypeStruct((TB, E), BF16), ja...  148 us

profile of v4, /device:TPU:4, one launch (start us, length us, event | category | flops | bytes accessed | tf_op | source)
XLA Modules:
  0.0 150.5 jit_solution(5222946057809843861)
XLA Ops:
  0.6 147.7 %flipout_layer.1 = (bf16[512,128]{1,0:T(8,128)(2,1)}, bf16[512,128]{1,0:T(8,128)(2,1)}, bf16[512,384]{1,0:T(8,128)(2,1)}, bf16[512,384]{1,0:T(8,128)(2,1)}) custom-call(bf16[512,128]{1,0:T(8,128)(2,1)} %tok.1, s32[512,128]{1,0:T(8,128)} %in_mask.1, s32[512,1,384]{2,1,0:T(1,128)} %out_mask.1, bf16[512,384]{1,0:T(8,128)(2,1)} %bitcast.4, ...), custom_call_target="tpu_custom_call" | custom-call | tf_op jit(solution)/shard_map/flipout_layer/pallas_call | solution.py:365
  148.3 2.2 %hand_over.1 = (bf16[512,128]{1,0:T(8,128)(2,1)}, bf16[512,128]{1,0:T(8,128)(2,1)}, bf16[512,384]{1,0:T(8,128)(2,1)}, bf16[512,384]{1,0:T(8,128)(2,1)}) custom-call(bf16[512,128]{1,0:T(8,128)(2,1)} %get-tuple-element.12.refs_0_, bf16[512,128]{1,0:T(8,128)(2,1)} %get-tuple-element.13.refs_1_, bf16[512,384]{1,0:T(8,128)(2,1)} %get-tuple-element.14.refs_2_, ...), custom_call_target="tpu_custom_call" | custom-call | tf_op jit(solution)/shard_map/hand_over/pallas_call | solution.py:426

commit v5 on v4

--- a/solution.py
+++ b/solution.py
@@ -172,6 +172,8 @@
     sc[...] = jnp.where(rows >= cols, nt(qb, kb), 0.0).astype(BF16)
     sct[...] = jnp.where(rows <= cols, nt(kb, qb), 0.0).astype(BF16)
     nu[...] = nn(sc[...], vb)
+    qt = jnp.transpose(q).astype(BF16)
+    up = gout[...].astype(F32)
     inc[...] = jnp.zeros_like(inc)
     for k in range(1, NZ):
         @pl.when(s >= k)
@@ -183,11 +185,9 @@
     num = nu[...] + nn(qb, inb)
     inv = lax.rsqrt(jnp.mean(num * num, axis=-1, keepdims=True) + EPSILON)
     normed = num * inv
-    att_out[...] = normed.astype(BF16)
-    up = gout[...].astype(F32)
     dn = inv * (up - normed * jnp.mean(up * normed, axis=-1, keepdims=True))
     dnb = dn.astype(BF16)
-    sus[...] = nn(jnp.transpose(q).astype(BF16), dnb).astype(BF16)
+    sus[...] = nn(qt, dnb).astype(BF16)
     for k in range(1, NZ):
         @pl.when(s >= k)
         def _():
@@ -227,6 +227,7 @@
             gp[e, m] = (gp[e, m].astype(F32) + rr[way, left, m].astype(F32)).astype(BF16)
         send_sum(way, left, m, part, rs_s.at[way, left - 1, m], rs_r.at[way, left - 1, m])
 
+    att_out[...] = normed.astype(BF16)
     ds[...] = jnp.where(rows >= cols, nt(dnb, vb), 0.0).astype(BF16)
     dq = (nn(ds[...], kb) + nt(dnb, inb)) * slope_q
     gt[query, :] = jnp.transpose(dq).astype(BF16)

time: 151 us -> 151 us (level)
  no operation moved by 1% of the time
where the time goes in v5:
time: 151 us; the launch traced here: 150 us
  Pallas kernels  150 us (99%)
    pallas_call x1, Pallas kernels, local(): pl.pallas_call(kernel, out_shape=(jax.ShapeDtypeStruct((TB, E), BF16), ja...  148 us

profile of v5, /device:TPU:4, one launch (start us, length us, event | category | flops | bytes accessed | tf_op | source)
XLA Modules:
  0.0 150.4 jit_solution(12135099579868312012)
XLA Ops:
  0.6 147.5 %flipout_layer.1 = (bf16[512,128]{1,0:T(8,128)(2,1)}, bf16[512,128]{1,0:T(8,128)(2,1)}, bf16[512,384]{1,0:T(8,128)(2,1)}, bf16[512,384]{1,0:T(8,128)(2,1)}) custom-call(bf16[512,128]{1,0:T(8,128)(2,1)} %tok.1, s32[512,128]{1,0:T(8,128)} %in_mask.1, s32[512,1,384]{2,1,0:T(1,128)} %out_mask.1, bf16[512,384]{1,0:T(8,128)(2,1)} %bitcast.4, ...), custom_call_target="tpu_custom_call" | custom-call | tf_op jit(solution)/shard_map/flipout_layer/pallas_call | solution.py:366
  148.1 2.2 %hand_over.1 = (bf16[512,128]{1,0:T(8,128)(2,1)}, bf16[512,128]{1,0:T(8,128)(2,1)}, bf16[512,384]{1,0:T(8,128)(2,1)}, bf16[512,384]{1,0:T(8,128)(2,1)}) custom-call(bf16[512,128]{1,0:T(8,128)(2,1)} %get-tuple-element.12.refs_0_, bf16[512,128]{1,0:T(8,128)(2,1)} %get-tuple-element.13.refs_1_, bf16[512,384]{1,0:T(8,128)(2,1)} %get-tuple-element.14.refs_2_, ...), custom_call_target="tpu_custom_call" | custom-call | tf_op jit(solution)/shard_map/hand_over/pallas_call | solution.py:427
